TPU v7x, 256 devices: a whole 4x4x8 slice. The times are simulated.
256 devices in a mesh: sample: 8 (over x_hi, y), space: 32 (over x_lo, z, core).
Axes of the slice: x: 4 (x_hi: 2, x_lo: 2; x = x_hi * 2 + x_lo), y: 4, z: 8, core: 2. Of those that a mesh axis runs over, the one named last changes fastest.
Arguments:
- activations: bfloat16 [8, 64, 8, 1024], P('sample', 'space'), may hold values from -100 to 100
- cotangent: bfloat16 [8, 64, 8, 2048], P('sample', 'space'), may hold values from -100 to 100
- weight: bfloat16 [128, 1728], replicated, may hold values from -0.15625 to 0.15625
- a_inverse: float32 [1728, 1728], P('space'), may hold values from -0.2 to 4.2, as said below
- g_inverse: float32 [128, 128], replicated, may hold values from -0.2 to 4.2, as said below
Outputs:
- outputs: bfloat16 [8, 64, 8, 2048], P('sample', 'space')
- input_grad: bfloat16 [8, 64, 8, 1024], P('sample', 'space')
- a_factor: float32 [1728, 1728], P('space')
- g_factor: float32 [128, 128], replicated
- update: float32 [128, 1728], P(None, 'space')
Inputs may be any that keep to these rules, and one draw needn't show every extreme that they name: `a_inverse`: symmetric. `g_inverse`: symmetric.
All inputs are finite; a program needn't handle non-finite values.
Results may differ from a plain program's by a relative error of at most 0.013.
Values may be sent and summed in bfloat16 or wider, within the bound.
A program may use at most 64 MiB of HBM per device.

v0:
```python
import jax
import jax.numpy as jnp
from jax import lax
from jax.sharding import PartitionSpec as P


def with_halo(block, sides, width):
    for axis, dim in sides:
        count = lax.axis_size(axis)
        forward = [(i, i + 1) for i in range(count - 1)]
        backward = [(target, source) for source, target in forward]
        low = lax.ppermute(
            lax.slice_in_dim(block, block.shape[dim] - width, None, axis=dim), axis, forward
        )
        high = lax.ppermute(lax.slice_in_dim(block, 0, width, axis=dim), axis, backward)
        block = jnp.concatenate([low, block, high], axis=dim)
    return block


def grid_patches(extended, planes, span_y, span_z, chans, mirror):
    volume = extended.reshape(planes + 2, span_y, span_z, chans)
    volume = jnp.pad(volume, ((0, 0), (1, 1), (1, 1), (0, 0)))
    pieces = []
    for shift_x in range(3):
        for shift_y in range(3):
            for shift_z in range(3):
                start_x = 2 - shift_x if mirror else shift_x
                start_y = 2 - shift_y if mirror else shift_y
                start_z = 2 - shift_z if mirror else shift_z
                pieces.append(
                    volume[
                        start_x : start_x + planes,
                        start_y : start_y + span_y,
                        start_z : start_z + span_z,
                        :,
                    ]
                )
    return jnp.concatenate(pieces, axis=-1).reshape(planes * span_y * span_z, 27 * chans)


def contract(left, right):
    return lax.dot_general(
        left, right, (((0,), (0,)), ((), ())), preferred_element_type=jnp.float32
    )


def shards(activations, cotangent, weight, a_inverse, g_inverse):
    planes = activations.shape[1]
    span_y = activations.shape[2]
    chans_out, kernel_cols = weight.shape
    chans_in = kernel_cols // 27
    span_z = activations.shape[3] // chans_in
    cells = planes * span_y * span_z
    extended = with_halo(activations, (("space", 1),), 1)
    patches = grid_patches(extended[0], planes, span_y, span_z, chans_in, False)
    result = jnp.dot(patches, weight.T, preferred_element_type=jnp.float32).astype(jnp.bfloat16)
    outputs = result.reshape(1, planes, span_y, span_z * chans_out)
    grad_extended = with_halo(cotangent, (("space", 1),), 1)
    flipped = (
        weight.reshape(chans_out, 27, chans_in).transpose(1, 0, 2).reshape(27 * chans_out, chans_in)
    )
    grad_patches = grid_patches(grad_extended[0], planes, span_y, span_z, chans_out, True)
    backward = jnp.dot(grad_patches, flipped, preferred_element_type=jnp.float32).astype(
        jnp.bfloat16
    )
    input_grad = backward.reshape(1, planes, span_y, span_z * chans_in)
    flat_grad = cotangent.reshape(cells, chans_out)
    cell_total = float(lax.axis_size("sample") * lax.axis_size("space") * cells)
    share = kernel_cols // lax.axis_size("space")
    device_row = lax.axis_index("space") * share
    g_part = contract(flat_grad, flat_grad)
    w_part = contract(flat_grad, patches)
    empty_rows = jnp.zeros((share, kernel_cols), jnp.float32)
    whole = lax.all_gather(activations, "space", axis=1, tiled=True)[0]
    padded = jnp.pad(whole, ((1, 1), (0, 0), (0, 0)))
    turns = 8
    span = whole.shape[0] // turns

    def add_block(step_index, running):
        block = lax.dynamic_slice_in_dim(padded, step_index * span, span + 2, 0)
        block_patches = grid_patches(block, span, span_y, span_z, chans_in, False)
        chosen = lax.dynamic_slice_in_dim(block_patches, device_row, share, 1)
        return running + contract(chosen, block_patches)

    a_rows = lax.fori_loop(0, turns, add_block, empty_rows)
    a_rows = lax.psum(a_rows.astype(jnp.bfloat16), "sample").astype(jnp.float32)
    a_factor = a_rows / cell_total
    g_sum, w_sum = lax.psum((g_part, w_part), ("sample", "space"))
    grad = w_sum / cell_total
    half_step = lax.dot_general(
        grad,
        a_inverse,
        (((1,), (1,)), ((), ())),
        precision=lax.Precision.HIGHEST,
        preferred_element_type=jnp.float32,
    )
    g_factor = g_sum / cell_total
    update = jnp.dot(g_inverse, half_step, precision=lax.Precision.HIGHEST)
    return (outputs, input_grad, a_factor, g_factor, update)


def solution(mesh):
    placed = (
        P("sample", "space", None, None),
        P("sample", "space", None, None),
        P(),
        P("space", None),
        P(),
    )
    return jax.shard_map(
        shards,
        mesh=mesh,
        in_specs=placed,
        out_specs=(
            P("sample", "space", None, None),
            P("sample", "space", None, None),
            P("space", None),
            P(),
            P(None, "space"),
        ),
        check_vma=False,
    )
```

profile of v0, /device:TPU:32, one launch (start us, length us, event | category | flops | bytes accessed | tf_op | source)
XLA Modules:
  0.0 519.4 jit_solution(1006859628336737487)
XLA Ops:
  10.8 3.6 collective-permute-start.1
  18.6 3.9 concatenate.229
  45.1 237.3 %all-reduce.10.cloned.1.call-done = (f32[128,128]{1,0:T(8,128)}, f32[128,1728]{0,1:T(8,128)}) async-done(((f32[128,128]{1,0:T(8,128)}, f32[128,1728]{0,1:T(8,128)}), (f32[128,128]{1,0:T(8,128)}, f32[128,1728]{0,1:T(8,128)})) %all-reduce.10.cloned.1.call-update) | async-done | bytes 950288 | tf_op jit(solution)/shard_map/psum | solution.py:88
  287.1 134.9 %while.16 = (s32[]{:T(128)}, f32[54,1728]{1,0:T(8,128)}, bf16[66,8,1024]{2,1,0:T(8,128)(2,1)S(1)}, s32[]{:T(128)}, s32[]{:T(128)}, /*index=5*/s32[]{:T(128)}, s32[]{:T(128)}, s32[]{:T(128)}, s32[]{}, s32[]{}) while((s32[]{:T(128)}, f32[54,1728]{1,0:T(8,128)}, bf16[66,8,1024]{2,1,0:T(8,128)(2,1)S(1)}, s32[]{:T(128)}, s32[]{:T(128)}, ...), condition=%wide.region_1.2_spmd.clone, body=%wide.region_0.1_spmd.clone.sunk | while | flops 191289600 | bytes 26137852 | solution.py:85
  291.6 8.5 %concatenate.296 = bf16[1024,1728]{1,0:T(8,128)(2,1)} concatenate(bf16[1024,64]{1,0:T(8,128)(2,1)S(1)} %bitcast.167, bf16[1024,64]{1,0:T(8,128)(2,1)S(1)} %bitcast.169, bf16[1024,64]{1,0:T(8,128)(2,1)} %bitcast.170, bf16[1024,64]{1,0:T(8,128)(2,1)} %bitcast.171, bf16[1024,64]{1,0:T(8,128)(2,1)S(1)} %concatenate.293, bf16[1024,64]{1,0:T(8,128)(2,1)} %bitcast.172, ...), dimensions={1} | concatenate | bytes 7077888 | tf_op jit(solution)/shard_map/while/body/eval_jaxpr/concatenate | solution.py:38
  300.1 3.8 convolution_add_fusion.2
  305.1 2.9 pad_slice_fusion.75
  308.4 8.5 %concatenate.296 = bf16[1024,1728]{1,0:T(8,128)(2,1)} concatenate(bf16[1024,64]{1,0:T(8,128)(2,1)S(1)} %bitcast.167, bf16[1024,64]{1,0:T(8,128)(2,1)S(1)} %bitcast.169, bf16[1024,64]{1,0:T(8,128)(2,1)} %bitcast.170, bf16[1024,64]{1,0:T(8,128)(2,1)} %bitcast.171, bf16[1024,64]{1,0:T(8,128)(2,1)S(1)} %concatenate.293, bf16[1024,64]{1,0:T(8,128)(2,1)} %bitcast.172, ...), dimensions={1} | concatenate | bytes 7077888 | tf_op jit(solution)/shard_map/while/body/eval_jaxpr/concatenate | solution.py:38
  316.9 3.9 convolution_add_fusion.2
  325.2 8.5 %concatenate.296 = bf16[1024,1728]{1,0:T(8,128)(2,1)} concatenate(bf16[1024,64]{1,0:T(8,128)(2,1)S(1)} %bitcast.167, bf16[1024,64]{1,0:T(8,128)(2,1)S(1)} %bitcast.169, bf16[1024,64]{1,0:T(8,128)(2,1)} %bitcast.170, bf16[1024,64]{1,0:T(8,128)(2,1)} %bitcast.171, bf16[1024,64]{1,0:T(8,128)(2,1)S(1)} %concatenate.293, bf16[1024,64]{1,0:T(8,128)(2,1)} %bitcast.172, ...), dimensions={1} | concatenate | bytes 7077888 | tf_op jit(solution)/shard_map/while/body/eval_jaxpr/concatenate | solution.py:38
  333.8 3.9 convolution_add_fusion.2
  342.1 8.5 %concatenate.296 = bf16[1024,1728]{1,0:T(8,128)(2,1)} concatenate(bf16[1024,64]{1,0:T(8,128)(2,1)S(1)} %bitcast.167, bf16[1024,64]{1,0:T(8,128)(2,1)S(1)} %bitcast.169, bf16[1024,64]{1,0:T(8,128)(2,1)} %bitcast.170, bf16[1024,64]{1,0:T(8,128)(2,1)} %bitcast.171, bf16[1024,64]{1,0:T(8,128)(2,1)S(1)} %concatenate.293, bf16[1024,64]{1,0:T(8,128)(2,1)} %bitcast.172, ...), dimensions={1} | concatenate | bytes 7077888 | tf_op jit(solution)/shard_map/while/body/eval_jaxpr/concatenate | solution.py:38
  350.6 3.9 convolution_add_fusion.2
  355.7 2.9 pad_slice_fusion.75
  359.0 8.5 %concatenate.296 = bf16[1024,1728]{1,0:T(8,128)(2,1)} concatenate(bf16[1024,64]{1,0:T(8,128)(2,1)S(1)} %bitcast.167, bf16[1024,64]{1,0:T(8,128)(2,1)S(1)} %bitcast.169, bf16[1024,64]{1,0:T(8,128)(2,1)} %bitcast.170, bf16[1024,64]{1,0:T(8,128)(2,1)} %bitcast.171, bf16[1024,64]{1,0:T(8,128)(2,1)S(1)} %concatenate.293, bf16[1024,64]{1,0:T(8,128)(2,1)} %bitcast.172, ...), dimensions={1} | concatenate | bytes 7077888 | tf_op jit(solution)/shard_map/while/body/eval_jaxpr/concatenate | solution.py:38
  367.5 3.9 convolution_add_fusion.2
  372.6 2.9 pad_slice_fusion.75
  375.8 8.5 %concatenate.296 = bf16[1024,1728]{1,0:T(8,128)(2,1)} concatenate(bf16[1024,64]{1,0:T(8,128)(2,1)S(1)} %bitcast.167, bf16[1024,64]{1,0:T(8,128)(2,1)S(1)} %bitcast.169, bf16[1024,64]{1,0:T(8,128)(2,1)} %bitcast.170, bf16[1024,64]{1,0:T(8,128)(2,1)} %bitcast.171, bf16[1024,64]{1,0:T(8,128)(2,1)S(1)} %concatenate.293, bf16[1024,64]{1,0:T(8,128)(2,1)} %bitcast.172, ...), dimensions={1} | concatenate | bytes 7077888 | tf_op jit(solution)/shard_map/while/body/eval_jaxpr/concatenate | solution.py:38
  384.4 3.9 convolution_add_fusion.2
  392.7 8.5 %concatenate.296 = bf16[1024,1728]{1,0:T(8,128)(2,1)} concatenate(bf16[1024,64]{1,0:T(8,128)(2,1)S(1)} %bitcast.167, bf16[1024,64]{1,0:T(8,128)(2,1)S(1)} %bitcast.169, bf16[1024,64]{1,0:T(8,128)(2,1)} %bitcast.170, bf16[1024,64]{1,0:T(8,128)(2,1)} %bitcast.171, bf16[1024,64]{1,0:T(8,128)(2,1)S(1)} %concatenate.293, bf16[1024,64]{1,0:T(8,128)(2,1)} %bitcast.172, ...), dimensions={1} | concatenate | bytes 7077888 | tf_op jit(solution)/shard_map/while/body/eval_jaxpr/concatenate | solution.py:38
  401.2 3.9 convolution_add_fusion.2
  409.6 8.5 %concatenate.296 = bf16[1024,1728]{1,0:T(8,128)(2,1)} concatenate(bf16[1024,64]{1,0:T(8,128)(2,1)S(1)} %bitcast.167, bf16[1024,64]{1,0:T(8,128)(2,1)S(1)} %bitcast.169, bf16[1024,64]{1,0:T(8,128)(2,1)} %bitcast.170, bf16[1024,64]{1,0:T(8,128)(2,1)} %bitcast.171, bf16[1024,64]{1,0:T(8,128)(2,1)S(1)} %concatenate.293, bf16[1024,64]{1,0:T(8,128)(2,1)} %bitcast.172, ...), dimensions={1} | concatenate | bytes 7077888 | tf_op jit(solution)/shard_map/while/body/eval_jaxpr/concatenate | solution.py:38
  418.1 3.9 convolution_add_fusion.2
  424.6 85.7 %all-reduce.8.cloned.1.call-done = bf16[54,1728]{1,0:T(8,128)(2,1)} async-done(((bf16[54,1728]{1,0:T(8,128)(2,1)}), bf16[54,1728]{1,0:T(8,128)(2,1)}) %all-reduce.8.cloned.1.call-update) | async-done | bytes 186640 | tf_op jit(solution)/shard_map/psum | solution.py:86
  (212 shorter events, 64.6 us)
Async XLA Ops:
  8.0 275.9 %copy-start = (f32[54,1728]{1,0:T(8,128)S(1)}, f32[54,1728]{1,0:T(8,128)}, u32[]{:S(2)}) copy-start(f32[54,1728]{1,0:T(8,128)} %param.10) | copy-start | bytes 1119748
  8.0 10.3 %copy-start.5 = (bf16[1,2,8,1024]{3,2,1,0:T(8,128)(2,1)S(1)}, bf16[1,2,8,1024]{3,2,1,0:T(8,128)(2,1)}, u32[]{:S(2)}) copy-start(bf16[1,2,8,1024]{3,2,1,0:T(8,128)(2,1)} %param.7) | copy-start | bytes 98308
  8.0 274.4 %all-reduce.10.cloned.1.call-start = ((), (), s32[]{:S(2)}) async-start(), calls=%async_computation.2 | async-start | bytes 1900544 | tf_op jit(solution)/shard_map/psum | solution.py:88
  8.9 8.2 %collective-permute-start = (bf16[1,1,8,1024]{3,2,1,0:T(8,128)(2,1)S(1)}, bf16[1,1,8,1024]{3,2,1,0:T(8,128)(2,1)S(1)}, u32[]{:S(2)}, u32[]{:S(2)}) collective-permute-start(bf16[1,1,8,1024]{3,2,1,0:T(8,128)(2,1)S(1)} %get-tuple-element.226), channel_id=1, source_target_pairs={{0,1},{1,2},{2,3},{3,4},{4,5},{5,6},{6,7},{7,8},{8,9},{9,10},{10,1... | collective-permute-start | bytes 49160 | tf_op jit(solution)/shard_map/ppermute | solution.py:12
  10.8 6.3 %collective-permute-start.1 = (bf16[1,1,8,1024]{3,2,1,0:T(8,128)(2,1)S(1)}, bf16[1,1,8,1024]{3,2,1,0:T(8,128)(2,1)S(1)}, u32[]{:S(2)}, u32[]{:S(2)}) collective-permute-start(bf16[1,1,8,1024]{3,2,1,0:T(8,128)(2,1)S(1)} %get-tuple-element.227), channel_id=1, source_target_pairs={{1,0},{2,1},{3,2},{4,3},{5,4},{6,5},{7,6},{8,7},{9,8},{10,9},{11,1... | collective-permute-start | bytes 49160 | tf_op jit(solution)/shard_map/ppermute | solution.py:15
  22.5 1.5 copy-start.4
  22.5 7.1 %copy-start.3 = (bf16[128,1728]{0,1:T(8,128)(2,1)S(1)}, bf16[128,1728]{0,1:T(8,128)(2,1)}, u32[]{:S(2)}) copy-start(bf16[128,1728]{0,1:T(8,128)(2,1)} %param.9) | copy-start | bytes 1327108
  23.9 261.9 %all-gather.2.cloned.1.call-start = ((), (), s32[]{:S(2)}) async-start(), calls=%async_computation | async-start | bytes 1081344 | tf_op jit(solution)/shard_map/all_gather | solution.py:74
  23.9 7.0 %collective-permute-start.2 = (bf16[1,1,8,2048]{3,2,1,0:T(8,128)(2,1)S(1)}, bf16[1,1,8,2048]{3,2,1,0:T(8,128)(2,1)S(1)}, u32[]{:S(2)}, u32[]{:S(2)}) collective-permute-start(bf16[1,1,8,2048]{3,2,1,0:T(8,128)(2,1)S(1)} %get-tuple-element.222), channel_id=1, source_target_pairs={{0,1},{1,2},{2,3},{3,4},{4,5},{5,6},{6,7},{7,8},{8,9},{9,10},{10,1... | collective-permute-start | bytes 98312 | tf_op jit(solution)/shard_map/ppermute | solution.py:12
  26.7 4.4 collective-permute-start.3
  29.6 480.7 %all-reduce.8.cloned.1.call-start = ((), (), s32[]{:S(2)}) async-start(), calls=%async_computation.1 | async-start | bytes 401408 | tf_op jit(solution)/shard_map/psum | solution.py:86
  33.1 9.1 %copy-start.9 = (bf16[2,8,16,128]{3,1,2,0:T(8,128)(2,1)S(1)}, bf16[2,8,16,128]{3,1,2,0:T(8,128)(2,1)}, u32[]{:S(2)}) copy-start(bf16[2,8,16,128]{3,1,2,0:T(8,128)(2,1)} %get-tuple-element.187) | copy-start | bytes 196612
  33.1 9.1 %copy-start.8 = (bf16[2,8,16,128]{3,1,2,0:T(8,128)(2,1)S(1)}, bf16[2,8,16,128]{3,1,2,0:T(8,128)(2,1)}, u32[]{:S(2)}) copy-start(bf16[2,8,16,128]{3,1,2,0:T(8,128)(2,1)} %get-tuple-element.188) | copy-start | bytes 196612
  34.0 8.2 %copy-start.7 = (bf16[2,8,16,128]{3,1,2,0:T(8,128)(2,1)S(1)}, bf16[2,8,16,128]{3,1,2,0:T(8,128)(2,1)}, u32[]{:S(2)}) copy-start(bf16[2,8,16,128]{3,1,2,0:T(8,128)(2,1)} %get-tuple-element.189) | copy-start | bytes 196612
  34.9 7.4 %copy-start.6 = (bf16[2,8,16,128]{3,1,2,0:T(8,128)(2,1)S(1)}, bf16[2,8,16,128]{3,1,2,0:T(8,128)(2,1)}, u32[]{:S(2)}) copy-start(bf16[2,8,16,128]{3,1,2,0:T(8,128)(2,1)} %get-tuple-element.190) | copy-start | bytes 196612
  287.1 136.6 %copy-start.12 = (f32[128,128]{1,0:T(8,128)S(1)}, f32[128,128]{1,0:T(8,128)}, u32[]{:S(2)}) copy-start(f32[128,128]{1,0:T(8,128)} %param.11) | copy-start | bytes 196612
  300.1 3.8 copy-start.2
  316.9 3.9 copy-start.2
  333.8 3.9 copy-start.2
  350.6 3.9 copy-start.2
  367.5 3.9 copy-start.2
  384.4 3.9 copy-start.2
  401.2 3.9 copy-start.2
  418.1 3.9 copy-start.2
  (10 other events, 10.3 us)
Sparse Core Ops, SparseCore 0:
  24.0 258.3 all-reduce.9
Sparse Core Ops, SparseCore 1:
  29.6 68.2 all-gather.1
  423.8 86.4 all-reduce.7
where the time goes:
time: 526 us; the launch traced here: 519 us
  waiting for transfers between devices  323 us (61%)
  local copies, waits for them, and re-layouts  125 us (24%)
  matrix products  36.7 us (7%)
  between operations  16.1 us (3%)
  starting transfers between devices  11.2 us (2%)
  other arithmetic  6.47 us (1%)
    psum x1, waiting for transfers between devices, shards(): g_sum, w_sum = lax.psum((g_part, w_part), ('sample', 'space'))  237 us
    psum x1, waiting for transfers between devices, shards(): a_rows = lax.psum(a_rows.astype(jnp.bfloat16), 'sample').astype(jnp.float32)  85.7 us
    concatenate x40, local copies, waits for them, and re-layouts, grid_patches(): jnp.concatenate(pieces, axis=-1)  78.5 us
    slice x52, local copies, waits for them, and re-layouts, grid_patches(): volume[start_x:start_x + planes, start_y:start_y + span_y, start_z:start_...  36.9 us
    dot_general x10, matrix products, contract(): lax.dot_general(left, right, (((0,), (0,)), ((), ())), preferred_element_...  33 us
  transfers between devices with their start and end apart: 7, of which 3 were waited for; matrix products, arithmetic and copies ran while one was open for 4% of the time, Pallas kernels for 0%

commit v1 on v0

v1 whole, which is shorter than its diff:
```python
import jax
import jax.numpy as jnp
from jax import lax
from jax.experimental import pallas as pl
from jax.experimental.pallas import tpu as pltpu
from jax.sharding import PartitionSpec as P

MESH = pl.DeviceIdType.MESH
F32 = jnp.float32
BF16 = jnp.bfloat16

CIN, COUT = 64, 128
NY, NZ = 8, 16
CELLS = NY * NZ
KC = 27 * CIN
ROWS = 9 * CIN
SHARE = KC // 32
HALF = 896
PLANES = 34
TOTAL = float(8 * 64 * CELLS)

Z_DELTAS = (1, 7, 2, 6, 3, 5, 4)
XY_DELTAS = tuple(
    sorted(
        ((a, b) for a in range(4) for b in range(4) if (a, b) != (0, 0)),
        key=lambda d: -(min(d[0], 4 - d[0]) + min(d[1], 4 - d[1])),
    )
)
SAMPLE_DELTAS = tuple(d for d in XY_DELTAS if d[0] % 2 == 0)


def nt(left, right):
    return lax.dot_general(left, right, (((1,), (1,)), ((), ())), preferred_element_type=F32)


def nn(left, right):
    return lax.dot_general(left, right, (((1,), (0,)), ((), ())), preferred_element_type=F32)


def tn(left, right):
    return lax.dot_general(left, right, (((0,), (0,)), ((), ())), preferred_element_type=F32)


def aligned(value, unit):
    return pl.multiple_of(value, unit)


def step_kernel(
    act_hbm, cot_hbm, weight_hbm, ainv_hbm,
    fin_ref, out_ref, igrad_ref, half_ref,
    planes, shifted, shift01, chosen, acc, rows_tmp, cells_tmp, cot_t, act_ref, cot_ref, weight_t, ainv_ref, load,
    send_a, recv_a, fin, send_g, recv_g, zsend, zrecv, quarters, hg,
    z_s, z_r, f_s, f_r, b_s, b_r, bf_s, bf_r, c_s, c_r,
    g_s, g_r, q_s, q_r, k_s, k_r, u_s, u_r, a_s, a_r, v_s, v_r,
):
    j = lax.axis_index("sample")
    s = lax.axis_index("space")
    xh, y = j // 4, j % 4
    xl, z, core = s // 16, (s // 2) % 8, s % 2
    x = xh * 2 + xl

    def dev(dx=0, dy=0, dz=0, other=False):
        x2, y2, z2 = (x + dx) % 4, (y + dy) % 4, (z + dz) % 8
        c2 = 1 - core if other else core
        return {"sample": (x2 // 2) * 4 + y2, "space": ((x2 % 2) * 8 + z2) * 2 + c2}

    def at_space(s2):
        return {"sample": j, "space": s2}

    def copy(src, dst, ssem, rsem, device):
        return pltpu.make_async_remote_copy(
            src_ref=src, dst_ref=dst, send_sem=ssem, recv_sem=rsem,
            device_id=device, device_id_type=MESH,
        )

    across = at_space((s + 32 - 1 + 2 * core) % 32)
    xl_peer = at_space(((1 - xl) * 8 + z) * 2 + core)
    xl_other = at_space(((1 - xl) * 8 + z) * 2 + 1 - core)
    edge_sender = jnp.logical_and(z == 7 * (1 - xl), core == 1 - xl)
    edge_receiver = core == xl
    edge_slot = 33 * (1 - xl)
    near_edge = z == 7 * (1 - xl)

    loads = [
        pltpu.make_async_copy(src, dst, load.at[n])
        for n, (src, dst) in enumerate(
            ((act_hbm, act_ref), (cot_hbm, cot_ref), (weight_hbm, weight_t), (ainv_hbm, ainv_ref))
        )
    ]
    for c in loads:
        c.start()

    barrier = pltpu.get_barrier_semaphore()

    def greet(device):
        pl.semaphore_signal(barrier, inc=1, device_id=device, device_id_type=MESH)

    for d in Z_DELTAS:
        greet(dev(dz=d))
    for dx, dy in XY_DELTAS:
        greet(dev(dx, dy))
    greet(dev(other=True))
    greet(xl_other)
    greet(across)

    @pl.when(edge_receiver)
    def _():
        greet(at_space(((1 - xl) * 8 + 7 * xl) * 2 + core))

    mine = 1 + 4 * z + 2 * core
    loads[0].wait()
    loads[1].wait()
    for p in range(2):
        for zz in range(NZ):
            pair = act_ref[p, :, (zz // 2) * 128 : (zz // 2) * 128 + 128].astype(F32)
            if zz % 2:
                pair = pltpu.roll(pair, 64, 1)
            cells_tmp[p, pl.ds(zz, NY, stride=NZ), :] = pair
    for p in range(2):
        for zz in range(NZ):
            cells_tmp[2 + p, pl.ds(zz, NY, stride=NZ), :] = cot_ref[
                p, :, zz * 128 : zz * 128 + 128
            ].astype(F32)
    for p in range(2):
        planes[mine + p] = jnp.transpose(cells_tmp[p])[:CIN].astype(BF16)
        cot_t[1 + 2 * core + p] = jnp.transpose(cells_tmp[2 + p]).astype(BF16)

    src = lax.broadcasted_iota(jnp.int32, (CELLS, CELLS), 0)
    cell = lax.broadcasted_iota(jnp.int32, (CELLS, CELLS), 1)
    cy, cz = cell // NZ, cell % NZ
    for n in range(9):
        dy, dz = n // 3 - 1, n % 3 - 1
        inside = (cy + dy >= 0) & (cy + dy < NY) & (cz + dz >= 0) & (cz + dz < NZ)
        hit = inside & (src == cell + dy * NZ + dz)
        shift01[:, n * CELLS : (n + 1) * CELLS] = jnp.where(hit, 1.0, 0.0).astype(BF16)

    planes[33 * xl] = jnp.zeros((CIN, CELLS), BF16)

    def build(first, count):
        value = planes[pl.ds(first, count)].reshape(count * CIN, CELLS)
        moved = nn(value, shift01[...]).astype(BF16)
        for q in range(count):
            for n in range(9):
                shifted[pl.ds(aligned((first + q) * ROWS + n * CIN, 64), CIN), :] = moved[
                    q * CIN : (q + 1) * CIN, n * CELLS : (n + 1) * CELLS
                ]

    def put(first, count, ssem, rsem, device):
        ref = planes.at[pl.ds(first, count)]
        return copy(ref, ref, ssem, rsem, device)

    peers = len(Z_DELTAS) + len(XY_DELTAS) + 3
    pl.semaphore_wait(barrier, peers + jnp.where(edge_sender, 8, 0))

    cot_core = copy(
        cot_t.at[pl.ds(1 + 2 * core, 2)], cot_t.at[pl.ds(1 + 2 * core, 2)],
        c_s.at[0], c_r.at[0], dev(other=True),
    )
    cot_edge = copy(
        cot_t.at[1 + 3 * core], cot_t.at[5 * (1 - core)], c_s.at[1], c_r.at[1], across
    )
    z_out = []
    for n, d in enumerate(Z_DELTAS):
        z_out.append(put(mine, 2, z_s.at[n], z_r.at[n], dev(dz=d)))
    f_out = [put(mine, 2, f_s.at[0], f_r.at[0], dev(other=True))]

    def edge_copy(i):
        zz = (z + i) % 8
        return copy(
            planes.at[32 - 31 * xl], planes.at[33 * xl],
            b_s.at[i], b_r.at[0], at_space(((1 - xl) * 8 + zz) * 2 + core),
        )

    edge_order = (1, 0, 7, 2, 6, 3, 5, 4)
    f_out[0].start()
    z_out[0].start()
    z_out[1].start()

    @pl.when(edge_sender)
    def _():
        for i in edge_order:
            edge_copy(i).start()

    for c in z_out[2:]:
        c.start()
    cot_core.start()
    cot_edge.start()

    edge_forward = put(edge_slot, 1, bf_s.at[0], bf_r.at[0], dev(other=True))

    def edge_arrive():
        @pl.when(edge_receiver)
        def _():
            edge_copy(0).wait_recv()
            edge_forward.start()

        @pl.when(jnp.logical_not(edge_receiver))
        def _():
            edge_forward.wait_recv()

        build(edge_slot, 1)

    def from_chip(n):
        return 1 + 4 * ((z + 8 - Z_DELTAS[n]) % 8)

    def arrive(n):
        z_out[n].wait_recv()
        c = put(from_chip(n) + 2 * core, 2, f_s.at[n + 1], f_r.at[n + 1], dev(other=True))
        c.start()
        f_out.append(c)

    build(33 * xl, 1)
    build(mine, 2)
    f_out[0].wait_recv()
    build(1 + 4 * z + 2 * (1 - core), 2)
    arrive(0)
    arrive(1)
    build(from_chip(0) + 2 * core, 2)
    build(from_chip(1) + 2 * core, 2)
    f_out[1].wait_recv()
    f_out[2].wait_recv()
    build(from_chip(0) + 2 * (1 - core), 2)
    build(from_chip(1) + 2 * (1 - core), 2)

    @pl.when(near_edge)
    def _():
        edge_arrive()

    cot_core.wait_recv()
    cot_cat = jnp.concatenate([cot_t[1], cot_t[2], cot_t[3], cot_t[4]], axis=1)

    def patch_cat(first, offset):
        return jnp.concatenate(
            [
                shifted[pl.ds(aligned((first + i - 1) * ROWS + offset, 64), HALF), :]
                for i in range(4)
            ],
            axis=1,
        )

    w_part = nt(cot_cat, patch_cat(4 * z + 1, core * HALF)).astype(BF16)
    g_part = nt(cot_cat, cot_cat).astype(BF16)
    for r in range(8):
        send_g[0, r] = w_part[r * 16 : r * 16 + 16, :512]
        send_g[1, r, :, :384] = w_part[r * 16 : r * 16 + 16, 512:]
        send_g[1, r, :, 384:] = g_part[r * 16 : r * 16 + 16]
    g_out = []
    for n, (dx, dy) in enumerate(XY_DELTAS):
        x2, y2 = (x + dx) % 4, (y + dy) % 4
        c = copy(
            send_g.at[x2 % 2, (x2 // 2) * 4 + y2], recv_g.at[n],
            g_s.at[n], g_r.at[n], dev(dx, dy),
        )
        c.start()
        g_out.append(c)

    for n in range(2, 7):
        arrive(n)
        build(from_chip(n) + 2 * core, 2)
    for n in range(2, 7):
        f_out[n + 1].wait_recv()
        build(from_chip(n) + 2 * (1 - core), 2)

    @pl.when(jnp.logical_not(near_edge))
    def _():
        edge_arrive()

    first_row = SHARE * (2 * z + core)
    base = (first_row // 16) * 16
    off = first_row % 16

    def choose(i, carry):
        for t in range(2):
            start = aligned(i * ROWS + t * 16 * SHARE + base, 16)
            rows_tmp[t] = shifted[pl.ds(start, 80), :].astype(F32)
            chosen[i, t * 64 : t * 64 + 64, :] = rows_tmp[t, pl.ds(off, 64), :].astype(BF16)
        return carry

    lax.fori_loop(0, 32, choose, 0)

    a_out = []

    def covariance(h):
        def body(i, carry):
            left = jnp.concatenate([chosen[4 * i + q] for q in range(4)], axis=1)
            acc[h] += nt(left, patch_cat(4 * i + 1, h * HALF))
            return carry

        acc[h] = jnp.zeros((128, HALF), F32)
        lax.fori_loop(0, 8, body, 0)
        for t in range(2):
            for q in range(4):
                send_a[t, 2 * q + h] = acc[h, t * 64 + q * 16 : t * 64 + q * 16 + 16].astype(BF16)

    covariance(0)
    covariance(1)
    for n, (dx, dy) in enumerate(XY_DELTAS):
        x2, y2 = (x + dx) % 4, (y + dy) % 4
        c = copy(
            send_a.at[x2 % 2, (x2 // 2) * 4 + y2], recv_a.at[n],
            a_s.at[n], a_r.at[n], dev(dx, dy),
        )
        c.start()
        a_out.append(c)

    total = send_g[xl, j].astype(F32)
    for n in range(15):
        g_out[n].wait_recv()
        total += recv_g[n].astype(F32)
    zsend[...] = total.astype(BF16)
    q_out = []
    for n, d in enumerate(Z_DELTAS):
        c = copy(zsend, zrecv.at[n], q_s.at[n], q_r.at[n], dev(dz=d))
        c.start()
        q_out.append(c)

    loads[2].wait()
    for p in range(2):
        patch = shifted[pl.ds(aligned((mine + p - 1) * ROWS, 64), KC), :]
        cells_tmp[p] = tn(patch, weight_t[...])
    for p in range(2):
        for zz in range(NZ):
            out_ref[p, :, zz * 128 : zz * 128 + 128] = cells_tmp[
                p, pl.ds(zz, NY, stride=NZ), :
            ].astype(BF16)

    cot_edge.wait_recv()

    @pl.when(s == 0)
    def _():
        cot_t[0] = jnp.zeros((COUT, CELLS), BF16)

    @pl.when(s == 31)
    def _():
        cot_t[5] = jnp.zeros((COUT, CELLS), BF16)

    w_cat = jnp.concatenate([weight_t[r * ROWS : (r + 1) * ROWS, :] for r in range(3)], axis=1)
    c64 = lax.broadcasted_iota(jnp.int32, (CIN, CELLS), 1)
    ly, lz = c64 // NZ, c64 % NZ
    for p in range(2):
        here = 1 + 2 * core + p
        c_cat = jnp.concatenate([cot_t[here + 1], cot_t[here], cot_t[here - 1]], axis=0)
        spread = nn(w_cat, c_cat)
        back = jnp.zeros((CIN, CELLS), F32)
        for n in range(9):
            dy, dz = n // 3 - 1, n % 3 - 1
            part = spread[n * CIN : (n + 1) * CIN]
            turn = (dy * NZ + dz) % CELLS
            if turn:
                part = pltpu.roll(part, turn, 1)
            inside = (ly - dy >= 0) & (ly - dy < NY) & (lz - dz >= 0) & (lz - dz < NZ)
            back += jnp.where(inside, part, 0.0)
        cells_tmp[2 + p] = jnp.transpose(jnp.concatenate([back, back], axis=0))
    lane = lax.broadcasted_iota(jnp.int32, (NY, 128), 1)
    for p in range(2):
        for zp in range(NZ // 2):
            even = cells_tmp[2 + p, pl.ds(2 * zp, NY, stride=NZ), :]
            odd = cells_tmp[2 + p, pl.ds(2 * zp + 1, NY, stride=NZ), :]
            igrad_ref[p, :, zp * 128 : zp * 128 + 128] = jnp.where(lane < 64, even, odd).astype(BF16)

    total = zsend[...].astype(F32)
    for n in range(7):
        q_out[n].wait_recv()
        total += zrecv[n].astype(F32)
    quarter = core * 2 + xl
    quarters[quarter] = total.astype(BF16)
    k_out = []
    for n, (device, other) in enumerate(
        ((xl_other, 3 - quarter), (xl_peer, core * 2 + 1 - xl), (dev(other=True), (1 - core) * 2 + xl))
    ):
        c = copy(quarters.at[quarter], quarters.at[quarter], k_s.at[n], k_r.at[n], device)
        c.start()
        k_out.append(c)
    loads[3].wait()
    ainv = ainv_ref[...]
    a_hi = ainv.astype(BF16)
    a_lo = (ainv - a_hi.astype(F32)).astype(BF16)

    piece = send_a[xl, j].astype(F32)
    for n in range(15):
        a_out[n].wait_recv()
        piece += recv_a[n].astype(F32)
    fin[j] = (piece * (1.0 / TOTAL)).astype(BF16)
    v_out = []
    for n, (dx, dy) in enumerate(SAMPLE_DELTAS):
        c = copy(fin.at[j], fin.at[j], v_s.at[n], v_r.at[n], dev(dx, dy))
        c.start()
        v_out.append(c)

    for c in k_out:
        c.wait_recv()
    grad = jnp.concatenate(
        [quarters[0], quarters[1, :, :384], quarters[2], quarters[3, :, :384]], axis=1
    )[:, :KC]
    half = (nt(grad, a_hi) + nt(grad, a_lo)) * (1.0 / TOTAL)
    hg[j, :, :128] = jnp.concatenate([half, jnp.zeros((16, 128 - SHARE), F32)], axis=1).astype(BF16)
    hg[j, :, 128:] = quarters[1, :, 384:]
    u_out = []
    for n, (dx, dy) in enumerate(SAMPLE_DELTAS):
        c = copy(hg.at[j], hg.at[j], u_s.at[n], u_r.at[n], dev(dx, dy))
        c.start()
        u_out.append(c)

    for c in v_out:
        c.wait_recv()
    fin_ref[...] = fin[...]
    for c in u_out:
        c.wait_recv()
    half_ref[...] = hg[...]

    for c in z_out + f_out + [cot_core, cot_edge] + g_out + q_out + k_out + a_out + v_out + u_out:
        c.wait_send()

    @pl.when(edge_receiver)
    def _():
        edge_forward.wait_send()

    @pl.when(edge_sender)
    def _():
        for i in range(8):
            edge_copy(i).wait_send()


def finish_kernel(
    fin_ref, out_in, igrad_in, hg_ref, ginv_ref, out_ref, igrad_ref, a_ref, g_ref, update_ref
):
    out_ref[...] = out_in[...]
    igrad_ref[...] = igrad_in[...]
    for q in range(4):
        deep = min(16, SHARE - 16 * q)
        a_ref[16 * q : 16 * q + deep, :HALF] = fin_ref[2 * q][:deep].astype(F32)
        a_ref[16 * q : 16 * q + deep, HALF:] = fin_ref[2 * q + 1][:deep, : KC - HALF].astype(F32)
    hg = hg_ref[...].reshape(COUT, 256)
    g_ref[...] = hg[:, 128:].astype(F32) * (1.0 / TOTAL)
    update = lax.dot_general(
        ginv_ref[...], hg[:, :128].astype(F32), (((1,), (0,)), ((), ())),
        precision=lax.Precision.HIGHEST, preferred_element_type=F32,
    )
    update_ref[...] = jnp.transpose(update)[:SHARE]


def shards(activations, cotangent, weight, a_inverse, g_inverse):
    vmem = pl.BlockSpec(memory_space=pltpu.VMEM)
    dma = pltpu.SemaphoreType.DMA
    counts = (7, 7, 8, 8, 8, 1, 1, 1, 2, 2, 15, 15, 7, 7, 3, 3, 7, 7, 15, 15, 7, 7)
    fin, outs, igrad, hg = pl.pallas_call(
        step_kernel,
        out_shape=(
            jax.ShapeDtypeStruct((8, 16, HALF), BF16),
            jax.ShapeDtypeStruct((2, NY, NZ * COUT), BF16),
            jax.ShapeDtypeStruct((2, NY, NZ * CIN), BF16),
            jax.ShapeDtypeStruct((8, 16, 256), BF16),
        ),
        in_specs=[pl.BlockSpec(memory_space=pltpu.HBM)] * 4,
        out_specs=[vmem] * 4,
        scratch_shapes=[
            pltpu.VMEM((PLANES, CIN, CELLS), BF16),
            pltpu.VMEM(((PLANES + 1) * ROWS, CELLS), BF16),
            pltpu.VMEM((CELLS, 9 * CELLS), BF16),
            pltpu.VMEM((32, 128, CELLS), BF16),
            pltpu.VMEM((2, 128, HALF), F32),
            pltpu.VMEM((2, 80, CELLS), F32),
            pltpu.VMEM((4, CELLS, 128), F32),
            pltpu.VMEM((6, COUT, CELLS), BF16),
            pltpu.VMEM((2, NY, NZ * CIN), BF16),
            pltpu.VMEM((2, NY, NZ * COUT), BF16),
            pltpu.VMEM((KC, COUT), BF16),
            pltpu.VMEM((SHARE, KC), F32),
            dma((4,)),
            pltpu.VMEM((2, 8, 16, HALF), BF16),
            pltpu.VMEM((15, 16, HALF), BF16),
            pltpu.VMEM((8, 16, HALF), BF16),
            pltpu.VMEM((2, 8, 16, 512), BF16),
            pltpu.VMEM((15, 16, 512), BF16),
            pltpu.VMEM((16, 512), BF16),
            pltpu.VMEM((7, 16, 512), BF16),
            pltpu.VMEM((4, 16, 512), BF16),
            pltpu.VMEM((8, 16, 256), BF16),
        ]
        + [dma((n,)) for n in counts],
        compiler_params=pltpu.CompilerParams(
            collective_id=0, has_side_effects=True, vmem_limit_bytes=63 << 20
        ),
        cost_estimate=pl.CostEstimate(flops=2 * 10**9, bytes_accessed=2 * 10**6, transcendentals=0),
        name="step",
    )(activations[0], cotangent[0], weight.T, a_inverse)
    outputs, input_grad, a_factor, g_factor, update = pl.pallas_call(
        finish_kernel,
        out_shape=(
            jax.ShapeDtypeStruct((2, NY, NZ * COUT), BF16),
            jax.ShapeDtypeStruct((2, NY, NZ * CIN), BF16),
            jax.ShapeDtypeStruct((SHARE, KC), F32),
            jax.ShapeDtypeStruct((COUT, COUT), F32),
            jax.ShapeDtypeStruct((SHARE, COUT), F32),
        ),
        in_specs=[vmem] * 5,
        out_specs=[vmem] * 5,
        compiler_params=pltpu.CompilerParams(vmem_limit_bytes=63 << 20),
        name="finish",
    )(fin, outs, igrad, hg, g_inverse)
    return outputs[None], input_grad[None], a_factor, g_factor, update.T


def solution(mesh):
    return jax.shard_map(
        shards,
        mesh=mesh,
        in_specs=(
            P("sample", "space", None, None),
            P("sample", "space", None, None),
            P(),
            P("space", None),
            P(),
        ),
        out_specs=(
            P("sample", "space", None, None),
            P("sample", "space", None, None),
            P("space", None),
            P(),
            P(None, "space"),
        ),
        check_vma=False,
    )
```

time: 526 us -> 49.5 us (0.09)
  the two profiles are of different devices: /device:TPU:32 before, /device:TPU:1 now
where the time goes in v1:
time: 49.5 us; the launch traced here: 49.3 us
  Pallas kernels  48.7 us (98%)
  between operations  0.64 us (1%)
    pallas_call x1, Pallas kernels, shards(): pl.pallas_call(step_kernel, out_shape=(jax.ShapeDtypeStruct((8, 16, HALF)...  46.7 us
    pallas_call x1, Pallas kernels, shards(): pl.pallas_call(finish_kernel, out_shape=(jax.ShapeDtypeStruct((2, NY, NZ...  2 us

profile of v1, /device:TPU:1, one launch (start us, length us, event | category | flops | bytes accessed | tf_op | source)
XLA Modules:
  0.0 49.3 jit_solution(11583214838968052455)
XLA Ops:
  0.6 46.7 %step.1 = (bf16[8,16,896]{2,1,0:T(8,128)(2,1)}, bf16[2,8,2048]{2,1,0:T(8,128)(2,1)}, bf16[2,8,1024]{2,1,0:T(8,128)(2,1)}, bf16[8,16,256]{2,1,0:T(8,128)(2,1)}) custom-call(bf16[2,8,1024]{2,1,0:T(8,128)(2,1)} %bitcast.9, bf16[2,8,2048]{2,1,0:T(8,128)(2,1)} %bitcast.7, bf16[1728,128]{1,0:T(8,128)(2,1)} %bitcast.6, f32[54,1728]{1,0:T(8,128)} %ainv_hbm.1), custom_call_target="tpu_custom_call" | custom-call | flops 2000000000 | bytes 2000000 | tf_op jit(solution)/shard_map/step/pallas_call | solution.py:446
  47.3 2.0 %finish.1 = (bf16[2,8,2048]{2,1,0:T(8,128)(2,1)}, bf16[2,8,1024]{2,1,0:T(8,128)(2,1)}, f32[54,1728]{1,0:T(8,128)}, f32[128,128]{1,0:T(8,128)}, f32[54,128]{1,0:T(8,128)}) custom-call(bf16[8,16,896]{2,1,0:T(8,128)(2,1)} %get-tuple-element.14.fin_ref, bf16[2,8,2048]{2,1,0:T(8,128)(2,1)} %get-tuple-element.15.out_in, ...), custom_call_target="tpu_custom_call" | custom-call | tf_op jit(solution)/shard_map/finish/pallas_call | solution.py:487

commit v2 on v1

--- a/solution.py
+++ b/solution.py
@@ -48,7 +48,7 @@
 def step_kernel(
     act_hbm, cot_hbm, weight_hbm, ainv_hbm,
     fin_ref, out_ref, igrad_ref, half_ref,
-    planes, shifted, shift01, chosen, acc, rows_tmp, cells_tmp, cot_t, act_ref, cot_ref, weight_t, ainv_ref, load,
+    planes, shifted, chosen, acc, side, rows_tmp, cells_tmp, cot_t, act_ref, cot_ref, weight_t, ainv_ref, load,
     send_a, recv_a, fin, send_g, recv_g, zsend, zrecv, quarters, hg,
     z_s, z_r, f_s, f_r, b_s, b_r, bf_s, bf_r, c_s, c_r,
     g_s, g_r, q_s, q_r, k_s, k_r, u_s, u_r, a_s, a_r, v_s, v_r,
@@ -79,7 +79,8 @@
     edge_sender = jnp.logical_and(z == 7 * (1 - xl), core == 1 - xl)
     edge_receiver = core == xl
     edge_slot = 33 * (1 - xl)
-    near_edge = z == 7 * (1 - xl)
+    edge_far = jnp.minimum((z + 1 - xl) % 8, (7 * (1 - xl) + 8 - z) % 8)
+    edge_far = jnp.minimum(edge_far, 3)
 
     loads = [
         pltpu.make_async_copy(src, dst, load.at[n])
@@ -125,25 +126,26 @@
         planes[mine + p] = jnp.transpose(cells_tmp[p])[:CIN].astype(BF16)
         cot_t[1 + 2 * core + p] = jnp.transpose(cells_tmp[2 + p]).astype(BF16)
 
-    src = lax.broadcasted_iota(jnp.int32, (CELLS, CELLS), 0)
-    cell = lax.broadcasted_iota(jnp.int32, (CELLS, CELLS), 1)
-    cy, cz = cell // NZ, cell % NZ
-    for n in range(9):
-        dy, dz = n // 3 - 1, n % 3 - 1
-        inside = (cy + dy >= 0) & (cy + dy < NY) & (cz + dz >= 0) & (cz + dz < NZ)
-        hit = inside & (src == cell + dy * NZ + dz)
-        shift01[:, n * CELLS : (n + 1) * CELLS] = jnp.where(hit, 1.0, 0.0).astype(BF16)
+    lane = lax.broadcasted_iota(jnp.int32, (CIN, CELLS), 1)
+    ly, lz = lane // NZ, lane % NZ
+
+    def within(dy, dz):
+        return (ly + dy >= 0) & (ly + dy < NY) & (lz + dz >= 0) & (lz + dz < NZ)
 
     planes[33 * xl] = jnp.zeros((CIN, CELLS), BF16)
 
+    def build_from(value, i):
+        for n in range(9):
+            dy, dz = n // 3 - 1, n % 3 - 1
+            turn = -(dy * NZ + dz) % CELLS
+            moved = pltpu.roll(value, turn, 1) if turn else value
+            shifted[pl.ds(aligned(i * ROWS + n * CIN, 64), CIN), :] = jnp.where(
+                within(dy, dz), moved, 0.0
+            ).astype(BF16)
+
     def build(first, count):
-        value = planes[pl.ds(first, count)].reshape(count * CIN, CELLS)
-        moved = nn(value, shift01[...]).astype(BF16)
         for q in range(count):
-            for n in range(9):
-                shifted[pl.ds(aligned((first + q) * ROWS + n * CIN, 64), CIN), :] = moved[
-                    q * CIN : (q + 1) * CIN, n * CELLS : (n + 1) * CELLS
-                ]
+            build_from(planes[first + q].astype(F32), first + q)
 
     def put(first, count, ssem, rsem, device):
         ref = planes.at[pl.ds(first, count)]
@@ -159,6 +161,7 @@
     cot_edge = copy(
         cot_t.at[1 + 3 * core], cot_t.at[5 * (1 - core)], c_s.at[1], c_r.at[1], across
     )
+    side_copy = copy(planes.at[mine + core], side, c_s.at[2], c_r.at[2], across)
     z_out = []
     for n, d in enumerate(Z_DELTAS):
         z_out.append(put(mine, 2, z_s.at[n], z_r.at[n], dev(dz=d)))
@@ -172,9 +175,11 @@
         )
 
     edge_order = (1, 0, 7, 2, 6, 3, 5, 4)
-    f_out[0].start()
     z_out[0].start()
     z_out[1].start()
+    side_copy.start()
+    f_out[0].start()
+    cot_core.start()
 
     @pl.when(edge_sender)
     def _():
@@ -183,22 +188,21 @@
 
     for c in z_out[2:]:
         c.start()
-    cot_core.start()
     cot_edge.start()
 
     edge_forward = put(edge_slot, 1, bf_s.at[0], bf_r.at[0], dev(other=True))
 
-    def edge_arrive():
-        @pl.when(edge_receiver)
+    def edge_arrive(level):
+        @pl.when(jnp.logical_and(edge_receiver, edge_far == level))
         def _():
             edge_copy(0).wait_recv()
             edge_forward.start()
-
-        @pl.when(jnp.logical_not(edge_receiver))
+            build(edge_slot, 1)
+
+        @pl.when(jnp.logical_and(jnp.logical_not(edge_receiver), jnp.maximum(edge_far, 1) == level))
         def _():
             edge_forward.wait_recv()
-
-        build(edge_slot, 1)
+            build(edge_slot, 1)
 
     def from_chip(n):
         return 1 + 4 * ((z + 8 - Z_DELTAS[n]) % 8)
@@ -215,16 +219,19 @@
     build(1 + 4 * z + 2 * (1 - core), 2)
     arrive(0)
     arrive(1)
-    build(from_chip(0) + 2 * core, 2)
-    build(from_chip(1) + 2 * core, 2)
-    f_out[1].wait_recv()
-    f_out[2].wait_recv()
-    build(from_chip(0) + 2 * (1 - core), 2)
-    build(from_chip(1) + 2 * (1 - core), 2)
-
-    @pl.when(near_edge)
-    def _():
-        edge_arrive()
+    beside = 4 * z + 5 * (1 - core)
+
+    @pl.when(jnp.logical_and(beside > 0, beside < 33))
+    def _():
+        build(beside, 1)
+
+    side_copy.wait_recv()
+
+    @pl.when(jnp.logical_and(s > 0, s < 31))
+    def _():
+        build_from(side[...].astype(F32), 4 * z + 5 * core)
+
+    edge_arrive(0)
 
     cot_core.wait_recv()
     cot_cat = jnp.concatenate([cot_t[1], cot_t[2], cot_t[3], cot_t[4]], axis=1)
@@ -254,54 +261,93 @@
         c.start()
         g_out.append(c)
 
-    for n in range(2, 7):
-        arrive(n)
-        build(from_chip(n) + 2 * core, 2)
-    for n in range(2, 7):
-        f_out[n + 1].wait_recv()
-        build(from_chip(n) + 2 * (1 - core), 2)
-
-    @pl.when(jnp.logical_not(near_edge))
-    def _():
-        edge_arrive()
-
     first_row = SHARE * (2 * z + core)
     base = (first_row // 16) * 16
     off = first_row % 16
 
     def choose(i, carry):
         for t in range(2):
-            start = aligned(i * ROWS + t * 16 * SHARE + base, 16)
+            start = aligned((i - 1) * ROWS + t * 16 * SHARE + base, 16)
             rows_tmp[t] = shifted[pl.ds(start, 80), :].astype(F32)
             chosen[i, t * 64 : t * 64 + 64, :] = rows_tmp[t, pl.ds(off, 64), :].astype(BF16)
         return carry
 
-    lax.fori_loop(0, 32, choose, 0)
+    chosen[0] = jnp.zeros((128, CELLS), BF16)
+    chosen[33] = jnp.zeros((128, CELLS), BF16)
+
+    def covariance(chips, fresh=False):
+        for chip in chips:
+            for i in range(6):
+                choose(jnp.clip(4 * chip + i, 1, 32), 0)
+        spots = [4 * chip + 1 + q for chip in chips for q in range(4)]
+        left = jnp.concatenate(
+            [shifted[pl.ds(aligned(i * ROWS, 64), ROWS), :] for i in spots], axis=1
+        )
+        right = jnp.concatenate(
+            [jnp.concatenate([chosen[i - k] for i in spots], axis=1) for k in (-1, 0, 1)], axis=0
+        )
+        if fresh:
+            acc[...] = nt(left, right)
+        else:
+            acc[...] += nt(left, right)
+
+    for n in range(2):
+        build(from_chip(n) + 2 * core, 2)
+    for n in range(2):
+        f_out[n + 1].wait_recv()
+        build(from_chip(n) + 2 * (1 - core), 2)
+    covariance((z,), fresh=True)
+    for level in (1, 2, 3):
+        news = (2, 3) if level == 1 else (4, 5) if level == 2 else (6,)
+        for n in news:
+            arrive(n)
+            build(from_chip(n) + 2 * core, 2)
+        for n in news:
+            f_out[n + 1].wait_recv()
+            build(from_chip(n) + 2 * (1 - core), 2)
+
+        edge_arrive(level)
+        near = ((z + 8 - level) % 8, (z + level) % 8)
+        covariance(near if level < 3 else near + ((z + 4) % 8,))
+
+    @pl.when(xl == 0)
+    def _():
+        acc[:, 256:] += nt(shifted[33 * ROWS : 34 * ROWS, :], chosen[32])
+
+    @pl.when(xl == 1)
+    def _():
+        acc[:, :128] += nt(shifted[:ROWS, :], chosen[1])
+
+    def column_tile(k):
+        parts = []
+        start, stop = 128 * k, min(128 * k + 128, KC)
+        while start < stop:
+            kx, row = start // ROWS, start % ROWS
+            deep = min(stop - start, ROWS - row)
+            parts.append(acc[row : row + deep, kx * 128 : kx * 128 + 128])
+            start += deep
+        return jnp.transpose(jnp.concatenate(parts, axis=0)).astype(BF16)
 
     a_out = []
-
-    def covariance(h):
-        def body(i, carry):
-            left = jnp.concatenate([chosen[4 * i + q] for q in range(4)], axis=1)
-            acc[h] += nt(left, patch_cat(4 * i + 1, h * HALF))
-            return carry
-
-        acc[h] = jnp.zeros((128, HALF), F32)
-        lax.fori_loop(0, 8, body, 0)
-        for t in range(2):
-            for q in range(4):
-                send_a[t, 2 * q + h] = acc[h, t * 64 + q * 16 : t * 64 + q * 16 + 16].astype(BF16)
-
-    covariance(0)
-    covariance(1)
     for n, (dx, dy) in enumerate(XY_DELTAS):
         x2, y2 = (x + dx) % 4, (y + dy) % 4
-        c = copy(
-            send_a.at[x2 % 2, (x2 // 2) * 4 + y2], recv_a.at[n],
-            a_s.at[n], a_r.at[n], dev(dx, dy),
-        )
-        c.start()
-        a_out.append(c)
+        a_out.append(
+            copy(
+                send_a.at[x2 % 2, (x2 // 2) * 4 + y2], recv_a.at[n],
+                a_s.at[n], a_r.at[n], dev(dx, dy),
+            )
+        )
+    for h in range(2):
+        for k in range(7):
+            tile = column_tile(7 * h + k)
+            wide = tile.shape[1]
+            for t in range(2):
+                for q in range(4):
+                    send_a[t, 2 * q + h, :, k * 128 : k * 128 + wide] = tile[
+                        t * 64 + q * 16 : t * 64 + q * 16 + 16
+                    ]
+    for c in a_out:
+        c.start()
 
     total = send_g[xl, j].astype(F32)
     for n in range(15):
@@ -335,8 +381,6 @@
         cot_t[5] = jnp.zeros((COUT, CELLS), BF16)
 
     w_cat = jnp.concatenate([weight_t[r * ROWS : (r + 1) * ROWS, :] for r in range(3)], axis=1)
-    c64 = lax.broadcasted_iota(jnp.int32, (CIN, CELLS), 1)
-    ly, lz = c64 // NZ, c64 % NZ
     for p in range(2):
         here = 1 + 2 * core + p
         c_cat = jnp.concatenate([cot_t[here + 1], cot_t[here], cot_t[here - 1]], axis=0)
@@ -348,15 +392,13 @@
             turn = (dy * NZ + dz) % CELLS
             if turn:
                 part = pltpu.roll(part, turn, 1)
-            inside = (ly - dy >= 0) & (ly - dy < NY) & (lz - dz >= 0) & (lz - dz < NZ)
-            back += jnp.where(inside, part, 0.0)
+            back += jnp.where(within(-dy, -dz), part, 0.0)
         cells_tmp[2 + p] = jnp.transpose(jnp.concatenate([back, back], axis=0))
-    lane = lax.broadcasted_iota(jnp.int32, (NY, 128), 1)
     for p in range(2):
         for zp in range(NZ // 2):
             even = cells_tmp[2 + p, pl.ds(2 * zp, NY, stride=NZ), :]
             odd = cells_tmp[2 + p, pl.ds(2 * zp + 1, NY, stride=NZ), :]
-            igrad_ref[p, :, zp * 128 : zp * 128 + 128] = jnp.where(lane < 64, even, odd).astype(BF16)
+            igrad_ref[p, :, zp * 128 : zp * 128 + 128] = jnp.where(lane[:NY] < 64, even, odd).astype(BF16)
 
     total = zsend[...].astype(F32)
     for n in range(7):
@@ -408,7 +450,7 @@
         c.wait_recv()
     half_ref[...] = hg[...]
 
-    for c in z_out + f_out + [cot_core, cot_edge] + g_out + q_out + k_out + a_out + v_out + u_out:
+    for c in z_out + f_out + [cot_core, cot_edge, side_copy] + g_out + q_out + k_out + a_out + v_out + u_out:
         c.wait_send()
 
     @pl.when(edge_receiver)
@@ -442,23 +484,23 @@
 def shards(activations, cotangent, weight, a_inverse, g_inverse):
     vmem = pl.BlockSpec(memory_space=pltpu.VMEM)
     dma = pltpu.SemaphoreType.DMA
-    counts = (7, 7, 8, 8, 8, 1, 1, 1, 2, 2, 15, 15, 7, 7, 3, 3, 7, 7, 15, 15, 7, 7)
+    counts = (7, 7, 8, 8, 8, 1, 1, 1, 3, 3, 15, 15, 7, 7, 3, 3, 7, 7, 15, 15, 7, 7)
     fin, outs, igrad, hg = pl.pallas_call(
         step_kernel,
         out_shape=(
-            jax.ShapeDtypeStruct((8, 16, HALF), BF16),
-            jax.ShapeDtypeStruct((2, NY, NZ * COUT), BF16),
-            jax.ShapeDtypeStruct((2, NY, NZ * CIN), BF16),
-            jax.ShapeDtypeStruct((8, 16, 256), BF16),
+            pltpu.VMEM((8, 16, HALF), BF16),
+            pltpu.VMEM((2, NY, NZ * COUT), BF16),
+            pltpu.VMEM((2, NY, NZ * CIN), BF16),
+            pltpu.VMEM((8, 16, 256), BF16),
         ),
         in_specs=[pl.BlockSpec(memory_space=pltpu.HBM)] * 4,
         out_specs=[vmem] * 4,
         scratch_shapes=[
             pltpu.VMEM((PLANES, CIN, CELLS), BF16),
             pltpu.VMEM(((PLANES + 1) * ROWS, CELLS), BF16),
-            pltpu.VMEM((CELLS, 9 * CELLS), BF16),
-            pltpu.VMEM((32, 128, CELLS), BF16),
-            pltpu.VMEM((2, 128, HALF), F32),
+            pltpu.VMEM((34, 128, CELLS), BF16),
+            pltpu.VMEM((ROWS, 384), F32),
+            pltpu.VMEM((CIN, CELLS), BF16),
             pltpu.VMEM((2, 80, CELLS), F32),
             pltpu.VMEM((4, CELLS, 128), F32),
             pltpu.VMEM((6, COUT, CELLS), BF16),
@@ -479,7 +521,7 @@
         ]
         + [dma((n,)) for n in counts],
         compiler_params=pltpu.CompilerParams(
-            collective_id=0, has_side_effects=True, vmem_limit_bytes=63 << 20
+            collective_id=0, has_side_effects=True, vmem_limit_bytes=58 << 20
         ),
         cost_estimate=pl.CostEstimate(flops=2 * 10**9, bytes_accessed=2 * 10**6, transcendentals=0),
         name="step",
@@ -495,7 +537,7 @@
         ),
         in_specs=[vmem] * 5,
         out_specs=[vmem] * 5,
-        compiler_params=pltpu.CompilerParams(vmem_limit_bytes=63 << 20),
+        compiler_params=pltpu.CompilerParams(vmem_limit_bytes=16 << 20),
         name="finish",
     )(fin, outs, igrad, hg, g_inverse)
     return outputs[None], input_grad[None], a_factor, g_factor, update.T

time: 49.5 us -> 42.3 us (0.85)
  Pallas kernels: 48.7 us -> 41.5 us
    pallas_call x1, Pallas kernels: 46.7 us -> 40.6 us  [shards(): pl.pallas_call(step_kernel, out_shape=(pltpu.VMEM((8, 16, HALF), BF16), p...]
    pallas_call x1, Pallas kernels: 2 us -> 0.97 us  [shards(): pl.pallas_call(finish_kernel, out_shape=(jax.ShapeDtypeStruct((2, NY, NZ...]
where the time goes in v2:
time: 42.3 us; the launch traced here: 42.2 us
  Pallas kernels  41.5 us (98%)
  between operations  0.66 us (2%)
    pallas_call x1, Pallas kernels, shards(): pl.pallas_call(step_kernel, out_shape=(pltpu.VMEM((8, 16, HALF), BF16), p...  40.6 us
    pallas_call x1, Pallas kernels, shards(): pl.pallas_call(finish_kernel, out_shape=(jax.ShapeDtypeStruct((2, NY, NZ...  0.97 us

profile of v2, /device:TPU:1, one launch (start us, length us, event | category | flops | bytes accessed | tf_op | source)
XLA Modules:
  0.0 42.2 jit_solution(8294096900847569664)
XLA Ops:
  0.6 0.0 copy-start
  0.6 40.6 %step.1 = (bf16[8,16,896]{2,1,0:T(8,128)(2,1)S(1)}, bf16[2,8,2048]{2,1,0:T(8,128)(2,1)S(1)}, bf16[2,8,1024]{2,1,0:T(8,128)(2,1)S(1)}, bf16[8,16,256]{2,1,0:T(8,128)(2,1)S(1)}) custom-call(bf16[2,8,1024]{2,1,0:T(8,128)(2,1)} %bitcast.9, bf16[2,8,2048]{2,1,0:T(8,128)(2,1)} %bitcast.7, bf16[1728,128]{1,0:T(8,128)(2,1)} %bitcast.6, f32[54,1728]{1,0:T(8,128)} %ainv_hbm.1), custom_call_target="tpu_custom_call" | custom-call | flops 2000000000 | bytes 2000000 | tf_op jit(solution)/shard_map/step/pallas_call | solution.py:488
  41.2 0.0 copy-done
  41.2 1.0 %finish.1 = (bf16[2,8,2048]{2,1,0:T(8,128)(2,1)}, bf16[2,8,1024]{2,1,0:T(8,128)(2,1)}, f32[54,1728]{1,0:T(8,128)}, f32[128,128]{1,0:T(8,128)}, f32[54,128]{1,0:T(8,128)}) custom-call(bf16[8,16,896]{2,1,0:T(8,128)(2,1)S(1)} %get-tuple-element.14.fin_ref, bf16[2,8,2048]{2,1,0:T(8,128)(2,1)S(1)} %get-tuple-element.15.out_in, ...), custom_call_target="tpu_custom_call" | custom-call | tf_op jit(solution)/shard_map/finish/pallas_call | solution.py:529
Async XLA Ops:
  0.6 40.6 %copy-start = (f32[128,128]{1,0:T(8,128)S(1)}, f32[128,128]{1,0:T(8,128)}, u32[]{:S(2)}) copy-start(f32[128,128]{1,0:T(8,128)} %ginv_ref.1) | copy-start | bytes 196612

commit v3 on v2

--- a/solution.py
+++ b/solution.py
@@ -81,6 +81,7 @@
     edge_slot = 33 * (1 - xl)
     edge_far = jnp.minimum((z + 1 - xl) % 8, (7 * (1 - xl) + 8 - z) % 8)
     edge_far = jnp.minimum(edge_far, 3)
+    edge_soon = (edge_far + 1) // 2
 
     loads = [
         pltpu.make_async_copy(src, dst, load.at[n])
@@ -96,7 +97,7 @@
     def greet(device):
         pl.semaphore_signal(barrier, inc=1, device_id=device, device_id_type=MESH)
 
-    for d in Z_DELTAS:
+    for d in reversed(Z_DELTAS):
         greet(dev(dz=d))
     for dx, dy in XY_DELTAS:
         greet(dev(dx, dy))
@@ -193,7 +194,7 @@
     edge_forward = put(edge_slot, 1, bf_s.at[0], bf_r.at[0], dev(other=True))
 
     def edge_arrive(level):
-        @pl.when(jnp.logical_and(edge_receiver, edge_far == level))
+        @pl.when(jnp.logical_and(edge_receiver, edge_soon == level))
         def _():
             edge_copy(0).wait_recv()
             edge_forward.start()
@@ -291,24 +292,40 @@
         else:
             acc[...] += nt(left, right)
 
-    for n in range(2):
-        build(from_chip(n) + 2 * core, 2)
-    for n in range(2):
-        f_out[n + 1].wait_recv()
-        build(from_chip(n) + 2 * (1 - core), 2)
-    covariance((z,), fresh=True)
-    for level in (1, 2, 3):
-        news = (2, 3) if level == 1 else (4, 5) if level == 2 else (6,)
+    toward = 1 - 2 * core
+
+    def chip_at(d):
+        return (z + 8 + d * toward) % 8
+
+    def direct(*news):
         for n in news:
             arrive(n)
+        for n in news:
             build(from_chip(n) + 2 * core, 2)
+
+    def forwarded(*news):
         for n in news:
             f_out[n + 1].wait_recv()
+        for n in news:
             build(from_chip(n) + 2 * (1 - core), 2)
 
-        edge_arrive(level)
-        near = ((z + 8 - level) % 8, (z + level) % 8)
-        covariance(near if level < 3 else near + ((z + 4) % 8,))
+    arrive(2)
+    arrive(3)
+    for n in range(4):
+        build(from_chip(n) + 2 * core, 2)
+    forwarded(0, 1)
+    edge_arrive(1)
+    covariance((z, chip_at(1)), fresh=True)
+    direct(4, 5)
+    forwarded(2, 3)
+    edge_arrive(2)
+    covariance((chip_at(-1), chip_at(2)))
+    direct(6)
+    forwarded(4, 5)
+    edge_arrive(3)
+    covariance((chip_at(-2), chip_at(3)))
+    forwarded(6)
+    covariance((chip_at(-3), chip_at(4)))
 
     @pl.when(xl == 0)
     def _():

time: 42.3 us -> 40.8 us (0.965)
  Pallas kernels: 41.5 us -> 39.7 us
    pallas_call x1, Pallas kernels: 40.6 us -> 38.8 us  [shards(): pl.pallas_call(step_kernel, out_shape=(pltpu.VMEM((8, 16, HALF), BF16), p...]
where the time goes in v3:
time: 40.8 us; the launch traced here: 40.4 us
  Pallas kernels  39.7 us (97%)
  between operations  0.66 us (2%)
    pallas_call x1, Pallas kernels, shards(): pl.pallas_call(step_kernel, out_shape=(pltpu.VMEM((8, 16, HALF), BF16), p...  38.8 us
    pallas_call x1, Pallas kernels, shards(): pl.pallas_call(finish_kernel, out_shape=(jax.ShapeDtypeStruct((2, NY, NZ...  0.97 us

profile of v3, /device:TPU:1, one launch (start us, length us, event | category | flops | bytes accessed | tf_op | source)
XLA Modules:
  0.0 40.4 jit_solution(10264880259318109714)
XLA Ops:
  0.6 0.0 copy-start
  0.6 38.8 %step.1 = (bf16[8,16,896]{2,1,0:T(8,128)(2,1)S(1)}, bf16[2,8,2048]{2,1,0:T(8,128)(2,1)S(1)}, bf16[2,8,1024]{2,1,0:T(8,128)(2,1)S(1)}, bf16[8,16,256]{2,1,0:T(8,128)(2,1)S(1)}) custom-call(bf16[2,8,1024]{2,1,0:T(8,128)(2,1)} %bitcast.9, bf16[2,8,2048]{2,1,0:T(8,128)(2,1)} %bitcast.7, bf16[1728,128]{1,0:T(8,128)(2,1)} %bitcast.6, f32[54,1728]{1,0:T(8,128)} %ainv_hbm.1), custom_call_target="tpu_custom_call" | custom-call | flops 2000000000 | bytes 2000000 | tf_op jit(solution)/shard_map/step/pallas_call | solution.py:505
  39.4 0.0 copy-done
  39.4 1.0 %finish.1 = (bf16[2,8,2048]{2,1,0:T(8,128)(2,1)}, bf16[2,8,1024]{2,1,0:T(8,128)(2,1)}, f32[54,1728]{1,0:T(8,128)}, f32[128,128]{1,0:T(8,128)}, f32[54,128]{1,0:T(8,128)}) custom-call(bf16[8,16,896]{2,1,0:T(8,128)(2,1)S(1)} %get-tuple-element.14.fin_ref, bf16[2,8,2048]{2,1,0:T(8,128)(2,1)S(1)} %get-tuple-element.15.out_in, ...), custom_call_target="tpu_custom_call" | custom-call | tf_op jit(solution)/shard_map/finish/pallas_call | solution.py:546
Async XLA Ops:
  0.6 38.8 %copy-start = (f32[128,128]{1,0:T(8,128)S(1)}, f32[128,128]{1,0:T(8,128)}, u32[]{:S(2)}) copy-start(f32[128,128]{1,0:T(8,128)} %ginv_ref.1) | copy-start | bytes 196612

commit v4 on v3

--- a/solution.py
+++ b/solution.py
@@ -322,6 +322,17 @@
     covariance((chip_at(-1), chip_at(2)))
     direct(6)
     forwarded(4, 5)
+    total = send_g[xl, j].astype(F32)
+    for n in range(15):
+        g_out[n].wait_recv()
+        total += recv_g[n].astype(F32)
+    zsend[...] = total.astype(BF16)
+    q_out = []
+    for n, d in enumerate(Z_DELTAS):
+        c = copy(zsend, zrecv.at[n], q_s.at[n], q_r.at[n], dev(dz=d))
+        c.start()
+        q_out.append(c)
+
     edge_arrive(3)
     covariance((chip_at(-2), chip_at(3)))
     forwarded(6)
@@ -365,17 +376,6 @@
                     ]
     for c in a_out:
         c.start()
-
-    total = send_g[xl, j].astype(F32)
-    for n in range(15):
-        g_out[n].wait_recv()
-        total += recv_g[n].astype(F32)
-    zsend[...] = total.astype(BF16)
-    q_out = []
-    for n, d in enumerate(Z_DELTAS):
-        c = copy(zsend, zrecv.at[n], q_s.at[n], q_r.at[n], dev(dz=d))
-        c.start()
-        q_out.append(c)
 
     loads[2].wait()
     for p in range(2):

time: 40.8 us -> 39.5 us (0.968)
  Pallas kernels: 39.7 us -> 38.6 us
    pallas_call x1, Pallas kernels: 38.8 us -> 37.7 us  [shards(): pl.pallas_call(step_kernel, out_shape=(pltpu.VMEM((8, 16, HALF), BF16), p...]
where the time goes in v4:
time: 39.5 us; the launch traced here: 39.3 us
  Pallas kernels  38.6 us (98%)
  between operations  0.66 us (2%)
    pallas_call x1, Pallas kernels, shards(): pl.pallas_call(step_kernel, out_shape=(pltpu.VMEM((8, 16, HALF), BF16), p...  37.7 us
    pallas_call x1, Pallas kernels, shards(): pl.pallas_call(finish_kernel, out_shape=(jax.ShapeDtypeStruct((2, NY, NZ...  0.97 us

profile of v4, /device:TPU:1, one launch (start us, length us, event | category | flops | bytes accessed | tf_op | source)
XLA Modules:
  0.0 39.3 jit_solution(9593629096149512817)
XLA Ops:
  0.6 0.0 copy-start
  0.6 37.7 %step.1 = (bf16[8,16,896]{2,1,0:T(8,128)(2,1)S(1)}, bf16[2,8,2048]{2,1,0:T(8,128)(2,1)S(1)}, bf16[2,8,1024]{2,1,0:T(8,128)(2,1)S(1)}, bf16[8,16,256]{2,1,0:T(8,128)(2,1)S(1)}) custom-call(bf16[2,8,1024]{2,1,0:T(8,128)(2,1)} %bitcast.9, bf16[2,8,2048]{2,1,0:T(8,128)(2,1)} %bitcast.7, bf16[1728,128]{1,0:T(8,128)(2,1)} %bitcast.6, f32[54,1728]{1,0:T(8,128)} %ainv_hbm.1), custom_call_target="tpu_custom_call" | custom-call | flops 2000000000 | bytes 2000000 | tf_op jit(solution)/shard_map/step/pallas_call | solution.py:505
  38.3 0.0 copy-done
  38.3 1.0 %finish.1 = (bf16[2,8,2048]{2,1,0:T(8,128)(2,1)}, bf16[2,8,1024]{2,1,0:T(8,128)(2,1)}, f32[54,1728]{1,0:T(8,128)}, f32[128,128]{1,0:T(8,128)}, f32[54,128]{1,0:T(8,128)}) custom-call(bf16[8,16,896]{2,1,0:T(8,128)(2,1)S(1)} %get-tuple-element.14.fin_ref, bf16[2,8,2048]{2,1,0:T(8,128)(2,1)S(1)} %get-tuple-element.15.out_in, ...), custom_call_target="tpu_custom_call" | custom-call | tf_op jit(solution)/shard_map/finish/pallas_call | solution.py:546
Async XLA Ops:
  0.6 37.7 %copy-start = (f32[128,128]{1,0:T(8,128)S(1)}, f32[128,128]{1,0:T(8,128)}, u32[]{:S(2)}) copy-start(f32[128,128]{1,0:T(8,128)} %ginv_ref.1) | copy-start | bytes 196612

commit v5 on v4

--- a/solution.py
+++ b/solution.py
@@ -47,9 +47,9 @@
 
 def step_kernel(
     act_hbm, cot_hbm, weight_hbm, ainv_hbm,
-    fin_ref, out_ref, igrad_ref, half_ref,
+    fin, out_ref, igrad_ref, hg,
     planes, shifted, chosen, acc, side, rows_tmp, cells_tmp, cot_t, act_ref, cot_ref, weight_t, ainv_ref, load,
-    send_a, recv_a, fin, send_g, recv_g, zsend, zrecv, quarters, hg,
+    send_a, recv_a, send_g, recv_g, zsend, zrecv, quarters,
     z_s, z_r, f_s, f_r, b_s, b_r, bf_s, bf_r, c_s, c_r,
     g_s, g_r, q_s, q_r, k_s, k_r, u_s, u_r, a_s, a_r, v_s, v_r,
 ):
@@ -462,10 +462,8 @@
 
     for c in v_out:
         c.wait_recv()
-    fin_ref[...] = fin[...]
     for c in u_out:
         c.wait_recv()
-    half_ref[...] = hg[...]
 
     for c in z_out + f_out + [cot_core, cot_edge, side_copy] + g_out + q_out + k_out + a_out + v_out + u_out:
         c.wait_send()
@@ -528,13 +526,11 @@
             dma((4,)),
             pltpu.VMEM((2, 8, 16, HALF), BF16),
             pltpu.VMEM((15, 16, HALF), BF16),
-            pltpu.VMEM((8, 16, HALF), BF16),
             pltpu.VMEM((2, 8, 16, 512), BF16),
             pltpu.VMEM((15, 16, 512), BF16),
             pltpu.VMEM((16, 512), BF16),
             pltpu.VMEM((7, 16, 512), BF16),
             pltpu.VMEM((4, 16, 512), BF16),
-            pltpu.VMEM((8, 16, 256), BF16),
         ]
         + [dma((n,)) for n in counts],
         compiler_params=pltpu.CompilerParams(

time: 39.5 us -> 39.5 us (level)
  no operation moved by 1% of the time
where the time goes in v5:
time: 39.5 us; the launch traced here: 39.3 us
  Pallas kernels  38.6 us (98%)
  between operations  0.66 us (2%)
    pallas_call x1, Pallas kernels, shards(): pl.pallas_call(step_kernel, out_shape=(pltpu.VMEM((8, 16, HALF), BF16), p...  37.7 us
    pallas_call x1, Pallas kernels, shards(): pl.pallas_call(finish_kernel, out_shape=(jax.ShapeDtypeStruct((2, NY, NZ...  0.97 us

profile of v5, /device:TPU:1, one launch (start us, length us, event | category | flops | bytes accessed | tf_op | source)
XLA Modules:
  0.0 39.3 jit_solution(6323598483207204276)
XLA Ops:
  0.6 0.0 copy-start
  0.6 37.7 %step.1 = (bf16[8,16,896]{2,1,0:T(8,128)(2,1)S(1)}, bf16[2,8,2048]{2,1,0:T(8,128)(2,1)S(1)}, bf16[2,8,1024]{2,1,0:T(8,128)(2,1)S(1)}, bf16[8,16,256]{2,1,0:T(8,128)(2,1)S(1)}) custom-call(bf16[2,8,1024]{2,1,0:T(8,128)(2,1)} %bitcast.9, bf16[2,8,2048]{2,1,0:T(8,128)(2,1)} %bitcast.7, bf16[1728,128]{1,0:T(8,128)(2,1)} %bitcast.6, f32[54,1728]{1,0:T(8,128)} %ainv_hbm.1), custom_call_target="tpu_custom_call" | custom-call | flops 2000000000 | bytes 2000000 | tf_op jit(solution)/shard_map/step/pallas_call | solution.py:503
  38.3 0.0 copy-done
  38.3 1.0 %finish.1 = (bf16[2,8,2048]{2,1,0:T(8,128)(2,1)}, bf16[2,8,1024]{2,1,0:T(8,128)(2,1)}, f32[54,1728]{1,0:T(8,128)}, f32[128,128]{1,0:T(8,128)}, f32[54,128]{1,0:T(8,128)}) custom-call(bf16[8,16,896]{2,1,0:T(8,128)(2,1)S(1)} %get-tuple-element.14.fin_ref, bf16[2,8,2048]{2,1,0:T(8,128)(2,1)S(1)} %get-tuple-element.15.out_in, ...), custom_call_target="tpu_custom_call" | custom-call | tf_op jit(solution)/shard_map/finish/pallas_call | solution.py:542
Async XLA Ops:
  0.6 37.7 %copy-start = (f32[128,128]{1,0:T(8,128)S(1)}, f32[128,128]{1,0:T(8,128)}, u32[]{:S(2)}) copy-start(f32[128,128]{1,0:T(8,128)} %ginv_ref.1) | copy-start | bytes 196612
